TPU v7x, 32 devices: a whole 2x2x4 slice. The times are simulated.
32 devices in a mesh: expert: 4 (over x, core), hidden: 8 (over z, y).
Axes of the slice: x: 2, y: 2, z: 4, core: 2. Of those that a mesh axis runs over, the one named last changes fastest.
Arguments:
- hidden_in: bfloat16 [512, 6144], P(('expert', 'hidden')), may hold values from -6 to 6
- norm_gain: float32 [6144], replicated, may hold values from 0.25 to 1.75
- router_weight: bfloat16 [6144, 4], replicated, may hold values from -0.078125 to 0.078125
- expert_ids: int32 [512, 2], P(('expert', 'hidden')), may hold values from 0 to 3, all different within a row; in each aligned block of 16 rows (0 to 15, 16 to 31, ...) at most 12 rows name the same one
- gate_proj: bfloat16 [4, 6144, 8192], P('expert', None, 'hidden'), may hold values from -0.078125 to 0.078125
- up_proj: bfloat16 [4, 6144, 8192], P('expert', None, 'hidden'), may hold values from -0.078125 to 0.078125
- down_proj: bfloat16 [4, 8192, 6144], P('expert', 'hidden'), may hold values from -0.0625 to 0.0625
Outputs:
- layer_out: bfloat16 [512, 6144], P(('expert', 'hidden'))
Inputs may be any that keep to these rules, and one draw needn't show every extreme that they name: `expert_ids`: the two experts of a token differ. Within the rows of one device (aligned blocks of 16 tokens) no expert is named by more than 12 rows, a bound that some block reaches.
All inputs are finite; a program needn't handle non-finite values.
Results may differ from a plain program's by a relative error of at most 0.0085.
Values may be sent and summed in bfloat16 or wider, within the bound.
A program may use at most 128 MiB of HBM per device.

v0:
```python
import jax
import jax.numpy as jnp
from jax import lax
from jax.sharding import PartitionSpec as P


def normalize(hidden_in, norm_gain):
    values = hidden_in.astype(jnp.float32)
    factor = lax.rsqrt(jnp.mean(values * values, axis=-1, keepdims=True) + 1e-05)
    return (values * factor * norm_gain).astype(jnp.bfloat16)


def gate_weights(normed, router_weight, expert_ids, experts):
    logits = jnp.dot(normed, router_weight, preferred_element_type=jnp.float32)
    picks = expert_ids[:, :, None] == jnp.arange(experts, dtype=jnp.int32)[None, None, :]
    chosen = jnp.sum(jnp.where(picks, logits[:, None, :], 0.0), axis=-1)
    first = jax.nn.sigmoid(chosen[:, 0] - chosen[:, 1])
    return jnp.stack([first, 1.0 - first], axis=1)


def route_slots(block_ids, experts, capacity):
    flat_ids = block_ids.reshape(-1)
    onehot = (flat_ids[:, None] == jnp.arange(experts, dtype=jnp.int32)[None, :]).astype(jnp.int32)
    before = jnp.cumsum(onehot, axis=0) - onehot
    rank_in = jnp.sum(before * onehot, axis=1)
    slot_place = flat_ids * capacity + rank_in
    owners = jnp.arange(flat_ids.shape[0], dtype=jnp.int32) // block_ids.shape[1]
    slot_token = jnp.zeros((experts * capacity,), jnp.int32).at[slot_place].set(owners)
    filled = jnp.zeros((experts * capacity,), jnp.bfloat16).at[slot_place].set(1.0)
    return (slot_place, slot_token, filled)


def per_device(hidden_in, norm_gain, router_weight, expert_ids, gate_proj, up_proj, down_proj):
    experts = lax.axis_size("expert")
    tok_rows = hidden_in.shape[0]
    width = hidden_in.shape[1]
    top_count = expert_ids.shape[1]
    capacity = 3 * tok_rows * top_count // (2 * experts)
    normed = normalize(hidden_in, norm_gain)
    gates = gate_weights(normed, router_weight, expert_ids, experts)
    slot_place, slot_token, filled = route_slots(expert_ids, experts, capacity)
    outgoing = (jnp.take(normed, slot_token, axis=0) * filled[:, None]).reshape(
        experts, capacity, width
    )
    gate_local = gate_proj[0]
    up_local = up_proj[0]
    down_local = down_proj[0]
    arrived = lax.all_to_all(outgoing, "expert", split_axis=0, concat_axis=0, tiled=True)
    piece = lax.all_gather(arrived.reshape(experts * capacity, width), "hidden", axis=0, tiled=True)
    gate = jnp.dot(piece, gate_local, preferred_element_type=jnp.float32)
    upper = jnp.dot(piece, up_local, preferred_element_type=jnp.float32)
    inner = (jax.nn.silu(gate) * upper).astype(jnp.bfloat16)
    piece = inner
    own_rows = lax.psum_scatter(
        jnp.dot(piece, down_local, preferred_element_type=jnp.float32).astype(jnp.bfloat16),
        "hidden",
        scatter_dimension=0,
        tiled=True,
    )
    answers = own_rows.reshape(experts, capacity, width)
    returned = lax.all_to_all(answers, "expert", split_axis=0, concat_axis=0, tiled=True).reshape(
        experts * capacity, width
    )
    picked = (
        jnp.take(returned, slot_place, axis=0)
        .reshape(tok_rows, top_count, width)
        .astype(jnp.float32)
    )
    mixture = jnp.sum(gates[:, :, None] * picked, axis=1)
    return (hidden_in.astype(jnp.float32) + mixture).astype(jnp.bfloat16)


def solution(mesh):
    placed = (
        P(("expert", "hidden"), None),
        P(),
        P(),
        P(("expert", "hidden"), None),
        P("expert", None, "hidden"),
        P("expert", None, "hidden"),
        P("expert", "hidden", None),
    )
    return jax.shard_map(
        per_device,
        mesh=mesh,
        in_specs=placed,
        out_specs=P(("expert", "hidden"), None),
        check_vma=False,
    )
```

profile of v0, /device:TPU:0, one launch (start us, length us, event | category | flops | bytes accessed | tf_op | source)
XLA Modules:
  0.0 263.0 jit_solution(11852302662006517849)
XLA Ops:
  6.5 0.0 copy-start
  6.5 0.0 all-gather.2.cloned.1.call-start
  6.5 0.7 broadcast_multiply_fusion
  7.2 0.8 copy.25
  8.0 0.1 copy.28
  8.1 0.1 mul.76
  8.2 0.1 reshape.85
  8.3 0.1 fusion.18
  8.3 0.1 reduce_window_sum.11
  8.4 0.2 select_reduce_fusion
  8.6 0.0 copy-start.5
  8.6 0.0 copy-start.7
  8.6 0.7 scatter_custom_fusion
  9.3 1.1 fusion.14
  10.4 0.8 scatter_custom_fusion.1
  11.2 0.1 mul.77
  11.3 0.1 broadcast_in_dim.59
  11.4 0.0 copy-done.5
  11.4 0.0 copy-done.7
  11.4 1.0 fusion.16
  12.4 0.0 copy-start.1
  12.4 0.9 gather_fusion
  13.4 0.1 gather.13
  13.5 0.1 select_multiply_fusion
  13.6 15.7 %all_to_all.10 = bf16[4,12,6144]{2,1,0:T(8,128)(2,1)S(1)} all-to-all(bf16[4,12,6144]{2,1,0:T(8,128)(2,1)S(1)} %select_multiply_fusion), channel_id=1, replica_groups=mesh['expert'=4,'hidden'=8] {'expert'}, dimensions={0} | all-to-all | bytes 1179648 | tf_op jit(solution)/shard_map/all_to_all | solution.py:48
  29.3 0.0 copy-done.1
  29.3 0.9 reshape.86
  30.3 0.0 all-gather.2.cloned.1.call-update
  30.3 0.0 reduce-scatter.2.cloned.1.call-start
  30.3 80.3 %all-gather.2.cloned.1.call-done = bf16[384,6144]{1,0:T(8,128)(2,1)} async-done(((bf16[48,6144]{1,0:T(8,128)(2,1)}), bf16[384,6144]{1,0:T(8,128)(2,1)}) %all-gather.2.cloned.1.call-update) | async-done | bytes 4718608 | tf_op jit(solution)/shard_map/all_gather | solution.py:49
  110.7 9.4 %fusion.4 = f32[384,1024]{1,0:T(8,128)S(1)} fusion(bf16[384,6144]{1,0:T(8,128)(2,1)} %all-gather.2.cloned.1.call-done, bf16[1,6144,1024]{2,1,0:T(8,128)(2,1)} %param.11), kind=kOutput, calls=%fused_computation.8 | convolution fusion | flops 4831838208 | bytes 18874368 | tf_op jit(solution)/shard_map/dot_general | solution.py:50
  120.0 21.6 %fusion.6 = bf16[384,6144]{1,0:T(8,128)(2,1)} fusion(bf16[1,1024,6144]{2,1,0:T(8,128)(2,1)} %param.13, f32[384,1024]{1,0:T(8,128)S(1)} %fusion.4, bf16[384,6144]{1,0:T(8,128)(2,1)} %all-gather.2.cloned.1.call-done, bf16[1,6144,1024]{2,1,0:T(8,128)(2,1)} %param.12), kind=kOutput, calls=%fused_computation.10 | convolution fusion | flops 9668395008 | bytes 36175872 | tf_op jit(solution)/shard_map/dot_general | solution.py:55
  141.7 0.0 copy-start.6
  141.7 0.0 copy-start.4
  141.7 0.0 copy-start.2
  141.7 0.0 copy-start.8
  141.7 0.0 reduce-scatter.2.cloned.1.call-update
  141.7 0.6 copy-done.6
  142.3 0.1 reduce_sum.43
  142.4 0.1 copy.26
  142.5 0.0 copy-done.4
  142.5 0.1 copy.27
  142.6 0.0 copy-done
  142.6 0.0 copy-done.2
  142.6 0.2 fusion.25
  142.8 0.0 copy-start.3
  142.9 92.9 %reduce-scatter.2.cloned.1.call-done = bf16[48,6144]{1,0:T(8,128)(2,1)} async-done(((bf16[384,6144]{1,0:T(8,128)(2,1)}), bf16[48,6144]{1,0:T(8,128)(2,1)}) %reduce-scatter.2.cloned.1.call-update) | async-done | bytes 589840 | tf_op jit(solution)/shard_map/reduce_scatter | solution.py:54
  235.7 2.1 reshape.87
  237.8 3.5 %all-to-all-start.1 = ((bf16[4,12,6144]{2,1,0:T(8,128)(2,1)}), bf16[4,12,6144]{2,1,0:T(8,128)(2,1)S(1)}, u32[]{:S(2)}, u32[]{:S(2)}) async-start(bf16[4,12,6144]{2,1,0:T(8,128)(2,1)} %reshape.87), calls=%async_computation.2 | async-start | bytes 1572864 | tf_op jit(solution)/shard_map/all_to_all | solution.py:61
  241.4 0.1 copy.24
  241.4 0.0 copy-done.8
  241.5 11.5 %all-to-all-done.1 = bf16[4,12,6144]{2,1,0:T(8,128)(2,1)S(1)} async-done(((bf16[4,12,6144]{2,1,0:T(8,128)(2,1)}), bf16[4,12,6144]{2,1,0:T(8,128)(2,1)S(1)}, u32[]{:S(2)}, u32[]{:S(2)}) %all-to-all-start.1) | async-done | bytes 589856 | tf_op jit(solution)/shard_map/all_to_all | solution.py:61
  252.9 0.1 reshape.88
  253.1 0.8 gather_fusion.1
  253.9 0.3 gather.15
  254.2 1.2 multiply_reduce_fusion
  255.4 0.0 copy-done.3
  255.4 0.7 fusion.17
  (12 shorter events, 0.1 us)
Async XLA Ops:
  6.5 136.1 %copy-start = (bf16[6144,4]{0,1:T(4,128)(2,1)S(1)}, bf16[6144,4]{0,1:T(4,128)(2,1)}, u32[]{:S(2)}) copy-start(bf16[6144,4]{0,1:T(4,128)(2,1)} %param.9) | copy-start | bytes 147460
  6.5 104.1 %all-gather.2.cloned.1.call-start = ((), (), s32[]{:S(2)}) async-start(), calls=%async_computation.3 | async-start | bytes 5308416 | tf_op jit(solution)/shard_map/all_gather | solution.py:49
  8.6 2.8 %copy-start.5 = (s32[32]{0:T(128)}, s32[32]{0:T(128)S(1)}, u32[]{:S(2)}) copy-start(s32[32]{0:T(128)S(1)} %select_reduce_fusion) | copy-start | bytes 388
  8.6 2.8 %copy-start.7 = (s32[32]{0:T(128)}, s32[32]{0:T(128)S(1)}, u32[]{:S(2)}) copy-start(s32[32]{0:T(128)S(1)} %fusion.19) | copy-start | bytes 388
  12.4 16.9 %copy-start.1 = (bf16[16,6144]{1,0:T(8,128)(2,1)}, bf16[16,6144]{1,0:T(8,128)(2,1)S(1)}, u32[]{:S(2)}) copy-start(bf16[16,6144]{1,0:T(8,128)(2,1)S(1)} %fusion.16) | copy-start | bytes 589828
  30.3 205.5 %reduce-scatter.2.cloned.1.call-start = ((), (), s32[]{:S(2)}) async-start(), calls=%async_computation.4 | async-start | bytes 5308416 | tf_op jit(solution)/shard_map/reduce_scatter | solution.py:54
  141.7 0.7 copy-start.6
  141.7 0.8 copy-start.4
  141.7 1.0 copy-start.2
  141.7 99.8 %copy-start.8 = (s32[32]{0:T(128)S(1)}, s32[32]{0:T(128)}, u32[]{:S(2)}) copy-start(s32[32]{0:T(128)} %copy-done.7) | copy-start | bytes 388
  142.8 112.6 %copy-start.3 = (bf16[16,6144]{1,0:T(8,128)(2,1)S(1)}, bf16[16,6144]{1,0:T(8,128)(2,1)}, u32[]{:S(2)}) copy-start(bf16[16,6144]{1,0:T(8,128)(2,1)} %param.7) | copy-start | bytes 589828
  237.8 15.1 %all-to-all-start.1 = ((bf16[4,12,6144]{2,1,0:T(8,128)(2,1)}), bf16[4,12,6144]{2,1,0:T(8,128)(2,1)S(1)}, u32[]{:S(2)}, u32[]{:S(2)}) async-start(bf16[4,12,6144]{2,1,0:T(8,128)(2,1)} %reshape.87), calls=%async_computation.2 | async-start | bytes 1572864 | tf_op jit(solution)/shard_map/all_to_all | solution.py:61
Sparse Core Ops, SparseCore 0:
  30.4 80.1 all-gather.1
  141.8 93.8 reduce-scatter.1
where the time goes:
time: 263 us
  waiting for transfers between devices  185 us (70%)
  matrix products  31.2 us (12%)
  blocking collectives  15.7 us (6%)
  between operations  13.6 us (5%)
  local copies, waits for them, and re-layouts  8.9 us (3%)
  other arithmetic  5.34 us (2%)
  starting transfers between devices  3.54 us (1%)
    reduce_scatter x1, waiting for transfers between devices, per_device(): lax.psum_scatter(jnp.dot(piece, down_local, preferred_element_type=jnp.fl...  92.9 us
    all_gather x1, waiting for transfers between devices, per_device(): lax.all_gather(arrived.reshape(experts * capacity, width), 'hidden', axis...  80.3 us
    dot_general x1, matrix products, per_device(): jnp.dot(piece, down_local, preferred_element_type=jnp.float32)  21.6 us
    all_to_all x1, blocking collectives, per_device(): lax.all_to_all(outgoing, 'expert', split_axis=0, concat_axis=0, tiled=True)  15.7 us
    all_to_all x1, waiting for transfers between devices, per_device(): lax.all_to_all(answers, 'expert', split_axis=0, concat_axis=0, tiled=True)  11.5 us
    dot_general x1, matrix products, per_device(): gate = jnp.dot(piece, gate_local, preferred_element_type=jnp.float32)  9.37 us
  transfers between devices with their start and end apart: 3, of which 3 were waited for; matrix products, arithmetic and copies ran while one was open for 0% of the time, Pallas kernels for 0%

commit v1 on v0

--- a/solution.py
+++ b/solution.py
@@ -1,6 +1,10 @@
+import functools
+
 import jax
 import jax.numpy as jnp
 from jax import lax
+from jax.experimental import pallas as pl
+from jax.experimental.pallas import tpu as pltpu
 from jax.sharding import PartitionSpec as P
 
 
@@ -20,9 +24,9 @@
 
 def route_slots(block_ids, experts, capacity):
     flat_ids = block_ids.reshape(-1)
-    onehot = (flat_ids[:, None] == jnp.arange(experts, dtype=jnp.int32)[None, :]).astype(jnp.int32)
-    before = jnp.cumsum(onehot, axis=0) - onehot
-    rank_in = jnp.sum(before * onehot, axis=1)
+    count = jnp.arange(flat_ids.shape[0], dtype=jnp.int32)
+    alike = jnp.logical_and(flat_ids[:, None] == flat_ids[None, :], count[None, :] < count[:, None])
+    rank_in = jnp.sum(alike.astype(jnp.int32), axis=1)
     slot_place = flat_ids * capacity + rank_in
     owners = jnp.arange(flat_ids.shape[0], dtype=jnp.int32) // block_ids.shape[1]
     slot_token = jnp.zeros((experts * capacity,), jnp.int32).at[slot_place].set(owners)
@@ -30,7 +34,7 @@
     return (slot_place, slot_token, filled)
 
 
-def per_device(hidden_in, norm_gain, router_weight, expert_ids, gate_proj, up_proj, down_proj):
+def routed_plan(hidden_in, norm_gain, router_weight, expert_ids, gate_proj, up_proj, down_proj):
     experts = lax.axis_size("expert")
     tok_rows = hidden_in.shape[0]
     width = hidden_in.shape[1]
@@ -42,17 +46,13 @@
     outgoing = (jnp.take(normed, slot_token, axis=0) * filled[:, None]).reshape(
         experts, capacity, width
     )
-    gate_local = gate_proj[0]
-    up_local = up_proj[0]
-    down_local = down_proj[0]
     arrived = lax.all_to_all(outgoing, "expert", split_axis=0, concat_axis=0, tiled=True)
     piece = lax.all_gather(arrived.reshape(experts * capacity, width), "hidden", axis=0, tiled=True)
-    gate = jnp.dot(piece, gate_local, preferred_element_type=jnp.float32)
-    upper = jnp.dot(piece, up_local, preferred_element_type=jnp.float32)
+    gate = jnp.dot(piece, gate_proj[0], preferred_element_type=jnp.float32)
+    upper = jnp.dot(piece, up_proj[0], preferred_element_type=jnp.float32)
     inner = (jax.nn.silu(gate) * upper).astype(jnp.bfloat16)
-    piece = inner
     own_rows = lax.psum_scatter(
-        jnp.dot(piece, down_local, preferred_element_type=jnp.float32).astype(jnp.bfloat16),
+        jnp.dot(inner, down_proj[0], preferred_element_type=jnp.float32).astype(jnp.bfloat16),
         "hidden",
         scatter_dimension=0,
         tiled=True,
@@ -70,7 +70,275 @@
     return (hidden_in.astype(jnp.float32) + mixture).astype(jnp.bfloat16)
 
 
+LANES = 128
+
+
+def block_kernel(
+    experts, nz,
+    hid_ref, gain_ref, router_ref, ids_ref, wg_hbm, wu_hbm, wd_hbm,
+    out_ref,
+    wg, wu, wd, xs, act, part, from_sib, from_s, from_f, from_z,
+    w_sems, ag_send, ag_recv, rs_send, rs_recv,
+):
+    rows, width = hid_ref.shape
+    half = 4 * nz * rows
+    hidden_units = wg.shape[1]
+
+    def slot(s, plane, f, dz):
+        return ((s * 2 + plane) * 2 + f) * nz + dz
+
+    def at(number, count=1):
+        return pl.ds(number * rows, count * rows)
+
+    e = lax.axis_index("expert")
+    h = lax.axis_index("hidden")
+    core, x = e % 2, e // 2
+    z, y = h // 2, h % 2
+    e_other = (1 - x) * 2 + core
+    h_other = z * 2 + (1 - y)
+    first = (e * (1 - core) + e_other * core, h_other * (1 - core) + h * core)
+    second = (e_other * (1 - core) + e * core, h * (1 - core) + h_other * core)
+    sibling = (x * 2 + (1 - core), h)
+
+    def z_peer(step):
+        return (e, ((z + step) % nz) * 2 + y)
+
+    loads = []
+    for number, (source, target) in enumerate(((wg_hbm, wg), (wu_hbm, wu), (wd_hbm, wd))):
+        loads.append(pltpu.make_async_copy(source.at[0], target, w_sems.at[number]))
+        loads[-1].start()
+
+    barrier = pltpu.get_barrier_semaphore()
+    peers = [first, second, sibling] + [z_peer(step) for step in range(1, nz)]
+    for peer in peers:
+        pl.semaphore_signal(barrier, inc=1, device_id=peer, device_id_type=pl.DeviceIdType.MESH)
+
+    values = hid_ref[...].astype(jnp.float32)
+    factor = lax.rsqrt(jnp.mean(values * values, axis=-1, keepdims=True) + 1e-05)
+    normed = (values * factor * gain_ref[...]).astype(jnp.bfloat16)
+    xs[at(0), pl.ds(0, width)] = normed
+    wide = normed.astype(jnp.float32)
+    id0, id1 = ids_ref[:, 0:1], ids_ref[:, 1:2]
+    l0 = jnp.zeros((rows, 1), jnp.float32)
+    l1 = jnp.zeros((rows, 1), jnp.float32)
+    for k in range(experts):
+        logit = jnp.sum(wide * router_ref[k : k + 1, :].astype(jnp.float32), axis=-1, keepdims=True)
+        l0 = l0 + jnp.where(id0 == k, logit, 0.0)
+        l1 = l1 + jnp.where(id1 == k, logit, 0.0)
+    g0 = 1.0 / (1.0 + jnp.exp(l1 - l0))
+    g1 = 1.0 - g0
+    lane = lax.broadcasted_iota(jnp.int32, (rows, LANES), 1)
+    picked = lane % experts
+    shares = jnp.where(picked == id0, g0, 0.0) + jnp.where(picked == id1, g1, 0.0)
+    high = shares.astype(jnp.bfloat16)
+    low = (shares - high.astype(jnp.float32)).astype(jnp.bfloat16)
+    xs[at(0), pl.ds(width, LANES)] = jnp.where(
+        lane < experts, high.astype(jnp.float32),
+        jnp.where(lane < 2 * experts, low.astype(jnp.float32), 0.0),
+    ).astype(jnp.bfloat16)
+
+    pl.semaphore_wait(barrier, len(peers))
+
+    sends = []
+
+    def push(source_slot, target_slot, peer):
+        copy = pltpu.make_async_remote_copy(
+            src_ref=xs.at[at(source_slot)],
+            dst_ref=xs.at[at(target_slot)],
+            send_sem=ag_send.at[len(sends)],
+            recv_sem=ag_recv.at[target_slot],
+            device_id=peer,
+            device_id_type=pl.DeviceIdType.MESH,
+        )
+        copy.start()
+        sends.append(copy)
+
+    def arrived(number):
+        pltpu.make_async_copy(xs.at[at(number)], xs.at[at(number)], ag_recv.at[number]).wait()
+
+    for step in range(1, nz):
+        push(0, slot(0, 0, 0, nz - step), z_peer(step))
+    push(0, slot(0, 0, 1, 0), first)
+    push(0, slot(1, 0, 0, 0), second)
+    push(0, slot(0, 1, 0, 0), sibling)
+    for dz in range(1, nz):
+        here = slot(0, 0, 0, dz)
+        arrived(here)
+        push(here, slot(0, 0, 1, dz), first)
+        push(here, slot(1, 0, 0, dz), second)
+        push(here, slot(0, 1, 0, dz), sibling)
+    for dz in range(nz):
+        here = slot(0, 0, 1, dz)
+        arrived(here)
+        push(here, slot(1, 0, 1, dz), second)
+        push(here, slot(0, 1, 1, dz), sibling)
+    for f in range(2):
+        for dz in range(nz):
+            here = slot(1, 0, f, dz)
+            arrived(here)
+            push(here, slot(1, 1, f, dz), sibling)
+    for s in range(2):
+        for f in range(2):
+            for dz in range(nz):
+                arrived(slot(s, 1, f, dz))
+
+    loads[0].wait()
+    loads[1].wait()
+
+    def inner_half(start):
+        lane_h = lax.broadcasted_iota(jnp.int32, (half, LANES), 1)
+        tail = xs[pl.ds(start, half), pl.ds(width, LANES)].astype(jnp.float32)
+        mine = jnp.logical_and(lane_h % experts == e, lane_h < 2 * experts)
+        share = jnp.sum(jnp.where(mine, tail, 0.0), axis=-1, keepdims=True)
+
+        @pl.loop(0, hidden_units // 256)
+        def _(number):
+            columns = pl.ds(pl.multiple_of(number * 256, 256), 256)
+            block = xs[pl.ds(start, half), pl.ds(0, width)]
+            gate = jnp.dot(block, wg[:, columns], preferred_element_type=jnp.float32)
+            upper = jnp.dot(block, wu[:, columns], preferred_element_type=jnp.float32)
+            inner = gate / (1.0 + jnp.exp(-gate)) * upper * share
+            act[pl.ds(start, half), columns] = inner.astype(jnp.bfloat16)
+
+    def down_half(start):
+        @pl.loop(0, width // 512)
+        def _(number):
+            columns = pl.ds(pl.multiple_of(number * 512, 512), 512)
+            part[pl.ds(start, half), columns] = jnp.dot(
+                act[pl.ds(start, half), :], wd[:, columns], preferred_element_type=jnp.float32
+            ).astype(jnp.bfloat16)
+
+    inner_half(0)
+    inner_half(half)
+    loads[2].wait()
+
+    returns = []
+
+    def give(source, target, number, peer):
+        copy = pltpu.make_async_remote_copy(
+            src_ref=source,
+            dst_ref=target,
+            send_sem=rs_send.at[number],
+            recv_sem=rs_recv.at[number],
+            device_id=peer,
+            device_id_type=pl.DeviceIdType.MESH,
+        )
+        copy.start()
+        returns.append(copy)
+        return copy
+
+    def add(number, source):
+        part[at(number), :] = (
+            part[at(number), :].astype(jnp.float32) + source.astype(jnp.float32)
+        ).astype(jnp.bfloat16)
+
+    def to_sibling(s, f):
+        number = s * 2 + f
+        return give(
+            part.at[at(slot(s, 1, f, 0), nz)], from_sib.at[at(number * nz, nz)], number, sibling
+        )
+
+    down_half(half)
+    sib = {(1, f): to_sibling(1, f) for f in (1, 0)}
+    down_half(0)
+    for f in (1, 0):
+        sib[0, f] = to_sibling(0, f)
+    order = list(range(1, nz)) + [0]
+    over_s, over_f, over_z = {}, {}, {}
+    for f in (1, 0):
+        sib[1, f].wait_recv()
+        for dz in order:
+            here = slot(1, 0, f, dz)
+            add(here, from_sib[at((2 + f) * nz + dz), :])
+            number = f * nz + dz
+            over_s[f, dz] = give(part.at[at(here)], from_s.at[at(number)], 4 + number, second)
+    sib[0, 1].wait_recv()
+    for dz in order:
+        here = slot(0, 0, 1, dz)
+        add(here, from_sib[at(nz + dz), :])
+        over_s[1, dz].wait_recv()
+        add(here, from_s[at(nz + dz), :])
+        over_f[dz] = give(part.at[at(here)], from_f.at[at(dz)], 4 + 2 * nz + dz, first)
+    sib[0, 0].wait_recv()
+    for dz in order:
+        here = slot(0, 0, 0, dz)
+        add(here, from_sib[at(dz), :])
+        over_s[0, dz].wait_recv()
+        add(here, from_s[at(dz), :])
+        over_f[dz].wait_recv()
+        if dz:
+            add(here, from_f[at(dz), :])
+            over_z[dz] = give(
+                part.at[at(here)], from_z.at[at(nz - dz - 1)], 4 + 3 * nz + (nz - dz - 1), z_peer(dz)
+            )
+    total = part[at(slot(0, 0, 0, 0)), :].astype(jnp.float32) + from_f[at(0), :].astype(jnp.float32)
+    for dz in range(1, nz):
+        over_z[dz].wait_recv()
+        total = total + from_z[at(nz - dz - 1), :].astype(jnp.float32)
+    out_ref[...] = (hid_ref[...].astype(jnp.float32) + total).astype(out_ref.dtype)
+
+    for copy in sends + returns:
+        copy.wait_send()
+
+
+def gathered_plan(hidden_in, norm_gain, router_weight, expert_ids, gate_proj, up_proj, down_proj):
+    experts = lax.axis_size("expert")
+    nz = lax.axis_size("hidden") // 2
+    rows, width = hidden_in.shape
+    units = gate_proj.shape[2]
+    blocks = 8 * nz
+    total = blocks * rows
+    bf16 = jnp.bfloat16
+    vmem = pl.BlockSpec(memory_space=pltpu.VMEM)
+    hbm = pl.BlockSpec(memory_space=pl.ANY)
+    return pl.pallas_call(
+        functools.partial(block_kernel, experts, nz),
+        out_shape=jax.ShapeDtypeStruct((rows, width), bf16),
+        in_specs=[vmem] * 4 + [hbm] * 3,
+        out_specs=vmem,
+        scratch_shapes=[
+            pltpu.VMEM((width, units), bf16),
+            pltpu.VMEM((width, units), bf16),
+            pltpu.VMEM((units, width), bf16),
+            pltpu.VMEM((total, width + LANES), bf16),
+            pltpu.VMEM((total, units), bf16),
+            pltpu.VMEM((total, width), bf16),
+            pltpu.VMEM((total // 2, width), bf16),
+            pltpu.VMEM((total // 4, width), bf16),
+            pltpu.VMEM((nz * rows, width), bf16),
+            pltpu.VMEM(((nz - 1) * rows, width), bf16),
+            pltpu.SemaphoreType.DMA((3,)),
+            pltpu.SemaphoreType.DMA((blocks,)),
+            pltpu.SemaphoreType.DMA((blocks,)),
+            pltpu.SemaphoreType.DMA((4 + 4 * nz,)),
+            pltpu.SemaphoreType.DMA((4 + 4 * nz,)),
+        ],
+        compiler_params=pltpu.CompilerParams(
+            collective_id=0, has_side_effects=True, vmem_limit_bytes=62 * 1024 * 1024
+        ),
+        cost_estimate=pl.CostEstimate(
+            flops=6 * total * width * units,
+            bytes_accessed=6 * width * units,
+            transcendentals=total * units,
+        ),
+    )(
+        hidden_in, norm_gain.reshape(1, width), router_weight.T, expert_ids,
+        gate_proj, up_proj, down_proj,
+    )
+
+
 def solution(mesh):
+    experts, hidden = mesh.shape["expert"], mesh.shape["hidden"]
+
+    def per_device(*arrays):
+        tokens = experts * hidden * arrays[0].shape[0]
+        width, units = arrays[4].shape[1:]
+        held = 2 * width * (3 * units + 3 * tokens)
+        square = experts == 4 and hidden % 2 == 0
+        if square and held < 60 * 1024 * 1024:
+            return gathered_plan(*arrays)
+        return routed_plan(*arrays)
+
     placed = (
         P(("expert", "hidden"), None),
         P(),

time: 263 us -> 115 us (0.44)
  waiting for transfers between devices: 185 us -> 0 us
  Pallas kernels: 0 us -> 112 us
  matrix products: 31.2 us -> 0 us
  blocking collectives: 15.7 us -> 0 us
  between operations: 13.6 us -> 0.01 us
  local copies, waits for them, and re-layouts: 8.9 us -> 2.97 us
  other arithmetic: 5.34 us -> 0 us
  starting transfers between devices: 3.54 us -> 0 us
    pallas_call x0 -> x1, Pallas kernels: none -> 112 us  [gathered_plan(): pl.pallas_call(functools.partial(block_kernel, experts, nz), out_shape=ja...]
    reduce_scatter x1 -> x0, waiting for transfers between devices: 92.9 us -> none  [per_device(): lax.psum_scatter(jnp.dot(piece, down_local, preferred_element_type=jnp.fl...]
    all_gather x1 -> x0, waiting for transfers between devices: 80.3 us -> none  [per_device(): lax.all_gather(arrived.reshape(experts * capacity, width), 'hidden', axis...]
    dot_general x3 -> x0, matrix products: 31.2 us -> none  [the longest x1 21.6 us: per_device(): jnp.dot(piece, down_local, preferred_element_type=jnp.float32)]
    all_to_all x1 -> x0, blocking collectives: 15.7 us -> none  [per_device(): lax.all_to_all(outgoing, 'expert', split_axis=0, concat_axis=0, tiled=True)]
    all_to_all x1 -> x0, waiting for transfers between devices: 11.5 us -> none  [per_device(): lax.all_to_all(answers, 'expert', split_axis=0, concat_axis=0, tiled=True)]
    all_to_all x1 -> x0, starting transfers between devices: 3.49 us -> none  [per_device(): lax.all_to_all(answers, 'expert', split_axis=0, concat_axis=0, tiled=True)]
    reshape x4 -> x0, local copies, waits for them, and re-layouts: 3.26 us -> none  [the longest x1 2.08 us: per_device(): answers = own_rows.reshape(experts, capacity, width)]
  transfers between devices with their start and end apart: 3 -> 0, of which waited for: 3 -> 0; matrix products, arithmetic and copies ran while one was open for 0% -> 0% of each run, Pallas kernels for 0% -> 0%
where the time goes in v1:
time: 115 us
  Pallas kernels  112 us (97%)
  local copies, waits for them, and re-layouts  2.97 us (3%)
    pallas_call x1, Pallas kernels, gathered_plan(): pl.pallas_call(functools.partial(block_kernel, experts, nz), out_shape=ja...  112 us
    unnamed x2, local copies, waits for them, and re-layouts  2.97 us

profile of v1, /device:TPU:0, one launch (start us, length us, event | category | flops | bytes accessed | tf_op | source)
XLA Modules:
  0.0 114.6 jit_solution(14701367269890636594)
XLA Ops:
  0.0 1.4 %copy.8.ids_ref = s32[16,2]{1,0:T(8,128)} copy(s32[16,2]{0,1:T(2,128)} %param.10) | data formatting | bytes 256 | tf_op args[3]
  1.4 111.7 %shard_map.73 = bf16[16,6144]{1,0:T(8,128)(2,1)} custom-call(bf16[16,6144]{1,0:T(8,128)(2,1)} %hid_ref.1, f32[1,6144]{1,0:T(1,128)} %bitcast.3, bf16[4,6144]{1,0:T(4,128)(2,1)} %bitcast.2, s32[16,2]{1,0:T(8,128)} %copy.8.ids_ref, bf16[1,6144,1024]{2,1,0:T(8,128)(2,1)} %wg_hbm.1, bf16[1,6144,1024]{2,1,0:T(8,128)(2,1)} %wu_hbm.1, bf16[1,1024,6144]{2,1,0:T(8,128)(2,1)} %wd_hbm.1), custom_call_target="tpu_custom_call" | custom-call | flops 19327352832 | bytes 37748736 | tf_op jit(solution)/shard_map/pallas_call | solution.py:294
  113.0 1.6 %copy.10 = bf16[16,6144]{1,0:T(8,128)(2,1)} copy(bf16[16,6144]{1,0:T(8,128)(2,1)} %shard_map.73) | data formatting | bytes 393216

commit v2 on v1

--- a/solution.py
+++ b/solution.py
@@ -156,34 +156,23 @@
     def arrived(number):
         pltpu.make_async_copy(xs.at[at(number)], xs.at[at(number)], ag_recv.at[number]).wait()
 
-    for step in range(1, nz):
+    near = sorted(range(1, nz), key=lambda step: min(step, nz - step))
+    for step in near:
         push(0, slot(0, 0, 0, nz - step), z_peer(step))
     push(0, slot(0, 0, 1, 0), first)
     push(0, slot(1, 0, 0, 0), second)
     push(0, slot(0, 1, 0, 0), sibling)
-    for dz in range(1, nz):
+    for dz in near:
         here = slot(0, 0, 0, dz)
         arrived(here)
         push(here, slot(0, 0, 1, dz), first)
         push(here, slot(1, 0, 0, dz), second)
         push(here, slot(0, 1, 0, dz), sibling)
-    for dz in range(nz):
+    for dz in [0] + near:
         here = slot(0, 0, 1, dz)
         arrived(here)
         push(here, slot(1, 0, 1, dz), second)
         push(here, slot(0, 1, 1, dz), sibling)
-    for f in range(2):
-        for dz in range(nz):
-            here = slot(1, 0, f, dz)
-            arrived(here)
-            push(here, slot(1, 1, f, dz), sibling)
-    for s in range(2):
-        for f in range(2):
-            for dz in range(nz):
-                arrived(slot(s, 1, f, dz))
-
-    loads[0].wait()
-    loads[1].wait()
 
     def inner_half(start):
         lane_h = lax.broadcasted_iota(jnp.int32, (half, LANES), 1)
@@ -207,10 +196,6 @@
             part[pl.ds(start, half), columns] = jnp.dot(
                 act[pl.ds(start, half), :], wd[:, columns], preferred_element_type=jnp.float32
             ).astype(jnp.bfloat16)
-
-    inner_half(0)
-    inner_half(half)
-    loads[2].wait()
 
     returns = []
 
@@ -238,12 +223,28 @@
             part.at[at(slot(s, 1, f, 0), nz)], from_sib.at[at(number * nz, nz)], number, sibling
         )
 
+    for f in range(2):
+        for dz in [0] + near:
+            arrived(slot(0, 1, f, dz))
+    loads[0].wait()
+    loads[1].wait()
+    inner_half(0)
+    loads[2].wait()
+    down_half(0)
+    sib = {(0, f): to_sibling(0, f) for f in (1, 0)}
+    for f in range(2):
+        for dz in [0] + near:
+            here = slot(1, 0, f, dz)
+            arrived(here)
+            push(here, slot(1, 1, f, dz), sibling)
+    for f in range(2):
+        for dz in [0] + near:
+            arrived(slot(1, 1, f, dz))
+    inner_half(half)
     down_half(half)
-    sib = {(1, f): to_sibling(1, f) for f in (1, 0)}
-    down_half(0)
     for f in (1, 0):
-        sib[0, f] = to_sibling(0, f)
-    order = list(range(1, nz)) + [0]
+        sib[1, f] = to_sibling(1, f)
+    order = near[::-1] + [0]
     over_s, over_f, over_z = {}, {}, {}
     for f in (1, 0):
         sib[1, f].wait_recv()
@@ -252,17 +253,17 @@
             add(here, from_sib[at((2 + f) * nz + dz), :])
             number = f * nz + dz
             over_s[f, dz] = give(part.at[at(here)], from_s.at[at(number)], 4 + number, second)
-    sib[0, 1].wait_recv()
+    for f in (1, 0):
+        sib[0, f].wait_recv()
+        for dz in order:
+            add(slot(0, 0, f, dz), from_sib[at(f * nz + dz), :])
     for dz in order:
         here = slot(0, 0, 1, dz)
-        add(here, from_sib[at(nz + dz), :])
         over_s[1, dz].wait_recv()
         add(here, from_s[at(nz + dz), :])
         over_f[dz] = give(part.at[at(here)], from_f.at[at(dz)], 4 + 2 * nz + dz, first)
-    sib[0, 0].wait_recv()
     for dz in order:
         here = slot(0, 0, 0, dz)
-        add(here, from_sib[at(dz), :])
         over_s[0, dz].wait_recv()
         add(here, from_s[at(dz), :])
         over_f[dz].wait_recv()

time: 115 us -> 109 us (0.948)
  Pallas kernels: 112 us -> 106 us
    pallas_call x1, Pallas kernels: 112 us -> 106 us  [gathered_plan(): pl.pallas_call(functools.partial(block_kernel, experts, nz), out_shape=ja...]
where the time goes in v2:
time: 109 us
  Pallas kernels  106 us (97%)
  local copies, waits for them, and re-layouts  2.97 us (3%)
    pallas_call x1, Pallas kernels, gathered_plan(): pl.pallas_call(functools.partial(block_kernel, experts, nz), out_shape=ja...  106 us
    unnamed x2, local copies, waits for them, and re-layouts  2.97 us

profile of v2, /device:TPU:0, one launch (start us, length us, event | category | flops | bytes accessed | tf_op | source)
XLA Modules:
  0.0 109.0 jit_solution(14047648209245986541)
XLA Ops:
  0.0 1.4 %copy.8.ids_ref = s32[16,2]{1,0:T(8,128)} copy(s32[16,2]{0,1:T(2,128)} %param.10) | data formatting | bytes 256 | tf_op args[3]
  1.4 106.0 %shard_map.73 = bf16[16,6144]{1,0:T(8,128)(2,1)} custom-call(bf16[16,6144]{1,0:T(8,128)(2,1)} %hid_ref.1, f32[1,6144]{1,0:T(1,128)} %bitcast.3, bf16[4,6144]{1,0:T(4,128)(2,1)} %bitcast.2, s32[16,2]{1,0:T(8,128)} %copy.8.ids_ref, bf16[1,6144,1024]{2,1,0:T(8,128)(2,1)} %wg_hbm.1, bf16[1,6144,1024]{2,1,0:T(8,128)(2,1)} %wu_hbm.1, bf16[1,1024,6144]{2,1,0:T(8,128)(2,1)} %wd_hbm.1), custom_call_target="tpu_custom_call" | custom-call | flops 19327352832 | bytes 37748736 | tf_op jit(solution)/shard_map/pallas_call | solution.py:295
  107.3 1.6 %copy.10 = bf16[16,6144]{1,0:T(8,128)(2,1)} copy(bf16[16,6144]{1,0:T(8,128)(2,1)} %shard_map.73) | data formatting | bytes 393216

commit v3 on v2

--- a/solution.py
+++ b/solution.py
@@ -77,7 +77,7 @@
     experts, nz,
     hid_ref, gain_ref, router_ref, ids_ref, wg_hbm, wu_hbm, wd_hbm,
     out_ref,
-    wg, wu, wd, xs, act, part, from_sib, from_s, from_f, from_z,
+    wg, wu, wd, xs, act, part, from_sib, from_one, from_two, from_z,
     w_sems, ag_send, ag_recv, rs_send, rs_recv,
 ):
     rows, width = hid_ref.shape
@@ -237,6 +237,23 @@
             here = slot(1, 0, f, dz)
             arrived(here)
             push(here, slot(1, 1, f, dz), sibling)
+    order = near[::-1] + [0]
+    over_one, over_two, over_z = {}, {}, {}
+
+    def reduce_first(s):
+        sib[s, 1].wait_recv()
+        for dz in order:
+            here = slot(s, 0, 1, dz)
+            add(here, from_sib[at((2 * s + 1) * nz + dz), :])
+            number = s * nz + dz
+            over_one[s, dz] = give(part.at[at(here)], from_one.at[at(number)], 4 + number, first)
+
+    def reduce_own(s):
+        sib[s, 0].wait_recv()
+        for dz in order:
+            add(slot(s, 0, 0, dz), from_sib[at(2 * s * nz + dz), :])
+
+    reduce_first(0)
     for f in range(2):
         for dz in [0] + near:
             arrived(slot(1, 1, f, dz))
@@ -244,35 +261,26 @@
     down_half(half)
     for f in (1, 0):
         sib[1, f] = to_sibling(1, f)
-    order = near[::-1] + [0]
-    over_s, over_f, over_z = {}, {}, {}
-    for f in (1, 0):
-        sib[1, f].wait_recv()
-        for dz in order:
-            here = slot(1, 0, f, dz)
-            add(here, from_sib[at((2 + f) * nz + dz), :])
-            number = f * nz + dz
-            over_s[f, dz] = give(part.at[at(here)], from_s.at[at(number)], 4 + number, second)
-    for f in (1, 0):
-        sib[0, f].wait_recv()
-        for dz in order:
-            add(slot(0, 0, f, dz), from_sib[at(f * nz + dz), :])
+    reduce_first(1)
+    reduce_own(1)
+    reduce_own(0)
     for dz in order:
-        here = slot(0, 0, 1, dz)
-        over_s[1, dz].wait_recv()
-        add(here, from_s[at(nz + dz), :])
-        over_f[dz] = give(part.at[at(here)], from_f.at[at(dz)], 4 + 2 * nz + dz, first)
+        over_one[0, dz].wait_recv()
+        add(slot(0, 0, 0, dz), from_one[at(dz), :])
+    for dz in order:
+        here = slot(1, 0, 0, dz)
+        over_one[1, dz].wait_recv()
+        add(here, from_one[at(nz + dz), :])
+        over_two[dz] = give(part.at[at(here)], from_two.at[at(dz)], 4 + 2 * nz + dz, second)
     for dz in order:
         here = slot(0, 0, 0, dz)
-        over_s[0, dz].wait_recv()
-        add(here, from_s[at(dz), :])
-        over_f[dz].wait_recv()
+        over_two[dz].wait_recv()
         if dz:
-            add(here, from_f[at(dz), :])
+            add(here, from_two[at(dz), :])
             over_z[dz] = give(
                 part.at[at(here)], from_z.at[at(nz - dz - 1)], 4 + 3 * nz + (nz - dz - 1), z_peer(dz)
             )
-    total = part[at(slot(0, 0, 0, 0)), :].astype(jnp.float32) + from_f[at(0), :].astype(jnp.float32)
+    total = part[at(slot(0, 0, 0, 0)), :].astype(jnp.float32) + from_two[at(0), :].astype(jnp.float32)
     for dz in range(1, nz):
         over_z[dz].wait_recv()
         total = total + from_z[at(nz - dz - 1), :].astype(jnp.float32)

time: 109 us -> 103 us (0.945); the launches traced: 109 us -> 101 us
  Pallas kernels: 106 us -> 97.9 us
    pallas_call x1, Pallas kernels: 106 us -> 97.9 us  [gathered_plan(): pl.pallas_call(functools.partial(block_kernel, experts, nz), out_shape=ja...]
where the time goes in v3:
time: 103 us; the launch traced here: 101 us
  Pallas kernels  97.9 us (95%)
  local copies, waits for them, and re-layouts  2.97 us (3%)
    pallas_call x1, Pallas kernels, gathered_plan(): pl.pallas_call(functools.partial(block_kernel, experts, nz), out_shape=ja...  97.9 us
    unnamed x2, local copies, waits for them, and re-layouts  2.97 us

profile of v3, /device:TPU:0, one launch (start us, length us, event | category | flops | bytes accessed | tf_op | source)
XLA Modules:
  0.0 100.9 jit_solution(6867535159906813854)
XLA Ops:
  0.0 1.4 %copy.8.ids_ref = s32[16,2]{1,0:T(8,128)} copy(s32[16,2]{0,1:T(2,128)} %param.10) | data formatting | bytes 256 | tf_op args[3]
  1.4 97.9 %shard_map.73 = bf16[16,6144]{1,0:T(8,128)(2,1)} custom-call(bf16[16,6144]{1,0:T(8,128)(2,1)} %hid_ref.1, f32[1,6144]{1,0:T(1,128)} %bitcast.3, bf16[4,6144]{1,0:T(4,128)(2,1)} %bitcast.2, s32[16,2]{1,0:T(8,128)} %copy.8.ids_ref, bf16[1,6144,1024]{2,1,0:T(8,128)(2,1)} %wg_hbm.1, bf16[1,6144,1024]{2,1,0:T(8,128)(2,1)} %wu_hbm.1, bf16[1,1024,6144]{2,1,0:T(8,128)(2,1)} %wd_hbm.1), custom_call_target="tpu_custom_call" | custom-call | flops 19327352832 | bytes 37748736 | tf_op jit(solution)/shard_map/pallas_call | solution.py:303
  99.3 1.6 %copy.10 = bf16[16,6144]{1,0:T(8,128)(2,1)} copy(bf16[16,6144]{1,0:T(8,128)(2,1)} %shard_map.73) | data formatting | bytes 393216
